TPU v7x, 32 devices: a whole 2x2x4 slice. The times are simulated.
32 devices in a mesh: rep: 2 (over x), row: 4 (over z), patch: 4 (over y, core).
Axes of the slice: x: 2, y: 2, z: 4, core: 2. Of those that a mesh axis runs over, the one named last changes fastest.
Arguments:
- tokens: bfloat16 [64, 64, 1152], P(('rep', 'row'), 'patch'), parts along dimension 0, may hold values from -6 to 6
- modulation: float32 [3, 1152], replicated, may hold values from -4 to 4
- w_query: bfloat16 [1152, 1152], replicated, may hold values from -1 to 1
- w_keyval: bfloat16 [1152, 2304], replicated, may hold values from -0.1875 to 0.1875
- w_out: bfloat16 [1152, 1152], replicated, may hold values from -0.1875 to 0.1875
- stale_kv: bfloat16 [32, 32, 2304], P(('rep', 'row'), 'patch'), parts along dimension 0, may hold values from -24 to 24, as said below
Outputs:
- block_out: bfloat16 [64, 64, 1152], P(('rep', 'row'), 'patch'), parts along dimension 0
- fresh_kv: bfloat16 [32, 32, 2304], P(('rep', 'row'), 'patch'), parts along dimension 0
There are 2 independent parts, one for each index of `rep`. A program takes and returns all parts, laid end to end along the dimension named above; an argument that names none is the same for every part. Nothing has to cross between parts.
Inputs may be any that keep to these rules, and one draw needn't show every extreme that they name: `stale_kv`: pooled keys in the first 1152 entries of the last dimension, pooled values in the last 1152.
All inputs are finite; a program needn't handle non-finite values.
Results may differ from a plain program's by a relative error of at most 0.008.
Values may be sent and summed in bfloat16 or wider, within the bound.
A program may use at most 128 MiB of HBM per device.

v0:
```python
import math

import jax
import jax.numpy as jnp
from jax import lax
from jax.sharding import PartitionSpec as P

HEADS = 16
HEAD_DIM = 72


def modulate(tokens, modulation):
    values = tokens.astype(jnp.float32)
    center = jnp.mean(values, axis=-1, keepdims=True)
    spread = jnp.mean((values - center) ** 2, axis=-1, keepdims=True)
    normal = (values - center) / jnp.sqrt(spread + 1e-06)
    return (normal * (1.0 + modulation[1]) + modulation[0]).astype(jnp.bfloat16)


def attend(carry, queries, rows, keep):
    running, total, summed = carry
    count = rows.shape[0]
    width = rows.shape[1] // 2
    keys = rows[:, :width].reshape(count, HEADS, HEAD_DIM)
    values = rows[:, width:].reshape(count, HEADS, HEAD_DIM)
    scores = jnp.einsum("thd,nhd->htn", queries, keys, preferred_element_type=jnp.float32)
    scores = scores * (1.0 / math.sqrt(HEAD_DIM))
    if keep is not None:
        scores = jnp.where(keep[None, None, :], scores, -1e30)
    newest = jnp.maximum(running, jnp.max(scores, axis=-1))
    factor = jnp.exp(running - newest)
    expo = jnp.exp(scores - newest[:, :, None])
    total = total * factor + jnp.sum(expo, axis=-1)
    added = jnp.einsum(
        "htn,nhd->thd", expo.astype(jnp.bfloat16), values, preferred_element_type=jnp.float32
    )
    summed = summed * jnp.transpose(factor)[:, :, None] + added
    return (newest, total, summed)


def fold_keys(carry, queries, rows, keep=None):
    count = rows.shape[0]
    block = math.gcd(count, 1024)
    if block == count:
        return attend(carry, queries, rows, keep)
    stacked = rows.reshape(count // block, block, rows.shape[1])
    if keep is None:

        def step_block(state, item):
            return (attend(state, queries, item, None), None)

        result, unused = lax.scan(step_block, carry, stacked)
        return result
    keep_blocks = keep.reshape(count // block, block)

    def step_masked(state, item):
        return (attend(state, queries, item[0], item[1]), None)

    result, unused = lax.scan(step_masked, carry, (stacked, keep_blocks))
    return result


def on_device(tokens, modulation, w_query, w_keyval, w_out, stale_kv):
    grid_rows, grid_cols, width = tokens.shape
    tok_count = grid_rows * grid_cols
    pooled = tok_count // 4
    normed = modulate(tokens, modulation).reshape(tok_count, width)
    query = jnp.dot(normed, w_query, preferred_element_type=jnp.float32).astype(jnp.bfloat16)
    keyval = jnp.dot(normed, w_keyval, preferred_element_type=jnp.float32)
    fresh_kv = (
        keyval.reshape(grid_rows // 2, 2, grid_cols // 2, 2, 2 * width)
        .mean(axis=(1, 3))
        .astype(jnp.bfloat16)
    )
    fresh_flat = fresh_kv.reshape(pooled, 2 * width)
    stale_flat = stale_kv.reshape(pooled, 2 * width)
    queries = query.reshape(tok_count, HEADS, HEAD_DIM)
    initial = (
        jnp.full((HEADS, tok_count), -1e30, jnp.float32),
        jnp.zeros((HEADS, tok_count), jnp.float32),
        jnp.zeros((tok_count, HEADS, HEAD_DIM), jnp.float32),
    )
    own_group = lax.axis_index("row")
    carry = fold_keys(initial, queries, lax.all_gather(fresh_flat, "patch", axis=0, tiled=True))
    groups = lax.all_gather(stale_flat[None], "row", axis=0, tiled=True)
    group_count = groups.shape[0]
    others = jnp.arange(group_count, dtype=jnp.int32) != own_group
    piece = lax.all_gather(groups, "patch", axis=1, tiled=True)
    keep_rows = jnp.broadcast_to(others[:, None], (group_count, piece.shape[1])).reshape(-1)
    running, total, summed = fold_keys(carry, queries, piece.reshape(-1, 2 * width), keep_rows)
    total_rows = jnp.transpose(total)
    attended = (summed / total_rows[:, :, None]).reshape(tok_count, width).astype(jnp.bfloat16)
    projected = jnp.dot(attended, w_out, preferred_element_type=jnp.float32)
    block_out = tokens.reshape(tok_count, width).astype(jnp.float32) + modulation[2] * projected
    return (block_out.astype(jnp.bfloat16).reshape(grid_rows, grid_cols, width), fresh_kv)


def solution(mesh):
    return jax.shard_map(
        on_device,
        mesh=mesh,
        in_specs=(
            P(("rep", "row"), "patch", None),
            P(),
            P(),
            P(),
            P(),
            P(("rep", "row"), "patch", None),
        ),
        out_specs=(P(("rep", "row"), "patch", None), P(("rep", "row"), "patch", None)),
        check_vma=False,
    )
```

profile of v0, /device:TPU:1, one launch (start us, length us, event | category | flops | bytes accessed | tf_op | source)
XLA Modules:
  0.0 78.0 jit_solution(16647840950695856359)
XLA Ops:
  7.2 0.0 copy-start
  7.2 0.0 all-gather.2.cloned.1.call-start
  7.2 17.6 %all_gather.10 = bf16[4,32,2304]{2,1,0:T(8,128)(2,1)} all-gather(bf16[1,32,2304]{2,1,0:T(8,128)(2,1)} %bitcast.79), channel_id=1, replica_groups=mesh['rep'=2,'row'=4,'patch'=4] {'row'}, dimensions={0}, use_global_device_ids=true | all-gather | bytes 737280 | tf_op jit(solution)/shard_map/all_gather | solution.py:85
  24.8 0.0 all-gather.2.cloned.1.call-update
  24.8 0.9 %slice_reduce_fusion.1 = (f32[1152]{0:T(1024)S(1)}, f32[1152]{0:T(1024)S(1)}, f32[1152]{0:T(1024)S(1)}) fusion(f32[3,1152]{1,0:T(4,128)} %param.7), kind=kLoop, calls=%fused_computation.44 | loop fusion | flops 1152 | bytes 27648 | tf_op jit(solution)/shard_map/slice | solution.py:94
  25.7 1.1 %convert_reduce_fusion = f32[8,16]{1,0:T(8,128)S(1)} fusion(bf16[8,16,1152]{2,1,0:T(8,128)(2,1)} %param.6), kind=kLoop, calls=%fused_computation.31 | loop fusion | flops 294784 | bytes 295424 | tf_op jit(solution)/shard_map/reduce_sum | solution.py:14
  26.8 1.2 %multiply_reduce_fusion = f32[8,16]{1,0:T(8,128)S(1)} fusion(bf16[8,16,1152]{2,1,0:T(8,128)(2,1)} %param.6, f32[8,16]{1,0:T(8,128)S(1)} %broadcast_multiply_fusion), kind=kLoop, calls=%fused_computation.29 | loop fusion | flops 589696 | bytes 295936 | tf_op jit(solution)/shard_map/reduce_sum | solution.py:15
  28.0 1.2 %add_convert_fusion = bf16[8,16,1152]{2,1,0:T(8,128)(2,1)S(1)} fusion(bf16[8,16,1152]{2,1,0:T(8,128)(2,1)} %param.6, f32[1152]{0:T(1024)S(1)} %get-tuple-element.3, f32[1152]{0:T(1024)S(1)} %get-tuple-element.4, f32[8,16]{1,0:T(8,128)S(1)} %add_sqrt_fusion, f32[8,16]{1,0:T(8,128)S(1)} %broadcast_multiply_fusion), kind=kLoop, calls=%fused_computation.28 | loop fusion | flops 884736 | bytes 600064 | tf_op jit(solution)/shard_map/convert_element_type | solution.py:17
  29.2 0.0 copy-done
  29.2 0.6 convolution_convert_fusion
  29.8 0.1 dot_general.24
  29.9 0.2 copy.19
  30.1 4.5 %fusion.13 = f32[4,8,2304]{2,1,0:T(8,128)S(1)} fusion(bf16[1152,2304]{1,0:T(8,128)(2,1)} %param.9, bf16[4,2,8,2,1152]{4,3,2,1,0:T(2,128)(2,1)S(1)} %dot_general.24), kind=kOutput, calls=%fused_computation.17 | convolution fusion | flops 679698432 | bytes 5898240 | tf_op jit(solution)/shard_map/dot_general | solution.py:69
  34.6 14.8 %all_gather.9 = bf16[128,2304]{1,0:T(8,128)(2,1)S(1)} all-gather(bf16[32,2304]{1,0:T(8,128)(2,1)S(1)} %fusion.50), channel_id=1, replica_groups=mesh['rep'=2,'row'=4,'patch'=4] {'patch'}, dimensions={0}, use_global_device_ids=true | all-gather | bytes 737280 | tf_op jit(solution)/shard_map/all_gather | solution.py:84
  49.4 0.9 %fusion.38 = (bf16[128,1152]{1,0:T(8,128)(2,1)}, bf16[128,1152]{1,0:T(8,128)(2,1)}) fusion(bf16[128,2304]{1,0:T(8,128)(2,1)S(1)} %all_gather.9), kind=kLoop, calls=%fused_computation.54 | loop fusion | bytes 1179648 | tf_op jit(solution)/shard_map/slice | solution.py:25
  50.3 1.2 %copy.21 = bf16[128,1152]{0,1:T(8,128)(2,1)S(1)} copy(bf16[128,1152]{1,0:T(8,128)(2,1)} %get-tuple-element.10) | data formatting | bytes 589824 | tf_op jit(solution)/shard_map/slice | solution.py:24
  51.5 1.9 %copy.22 = bf16[128,1152]{0,1:T(8,128)(2,1)} copy(bf16[128,1152]{1,0:T(8,128)(2,1)} %get-tuple-element.9) | data formatting | bytes 589824 | tf_op jit(solution)/shard_map/slice | solution.py:25
  53.3 0.6 broadcast_bitcast_fusion
  53.9 1.4 %fusion.39 = (f32[16,128]{1,0:T(8,128)S(1)}, f32[16,128,128]{1,2,0:T(8,128)}) fusion(bf16[128,16,72]{0,2,1:T(8,128)(2,1)S(1)} %bitcast.70, bf16[128,16,72]{0,2,1:T(8,128)(2,1)S(1)} %bitcast.74), kind=kOutput, calls=%fused_computation.55 | convolution fusion | flops 38270976 | bytes 1646592 | tf_op jit(solution)/shard_map/thd,nhd->htn/dot_general | solution.py:26
  55.3 0.7 multiply_convert_fusion
  56.0 0.0 all-gather.2.cloned.1.call-done
  56.0 0.0 copy-start.6
  56.0 3.2 %fusion.37 = (bf16[512,1152]{1,0:T(8,128)(2,1)}, bf16[512,1152]{1,0:T(8,128)(2,1)}) fusion(bf16[512,2304]{1,0:T(8,128)(2,1)} %bitcast.73), kind=kLoop, calls=%fused_computation.53 | loop fusion | bytes 4718592 | tf_op jit(solution)/shard_map/slice | solution.py:24
  59.2 2.4 %copy.29 = bf16[512,1152]{0,1:T(8,128)(2,1)} copy(bf16[512,1152]{1,0:T(8,128)(2,1)} %get-tuple-element.8) | data formatting | bytes 2359296
  61.6 2.4 %copy.28 = bf16[512,1152]{0,1:T(8,128)(2,1)} copy(bf16[512,1152]{1,0:T(8,128)(2,1)} %get-tuple-element.7) | data formatting | bytes 2359296
  64.0 0.0 copy-done.6
  64.0 0.0 copy-start.4
  64.0 2.3 %fusion.2 = (f32[16,128]{1,0:T(8,128)S(1)}, f32[16,128,512]{2,1,0:T(8,128)S(1)}) fusion(pred[512]{0:T(512)(128)(4,1)S(1)} %copy-done.6, bf16[128,16,72]{0,2,1:T(8,128)(2,1)S(1)} %bitcast.71, bf16[512,16,72]{0,2,1:T(8,128)(2,1)} %bitcast.69), kind=kOutput, calls=%fused_computation.4 | convolution fusion | flops 154138624 | bytes 5677568 | tf_op jit(solution)/shard_map/thd,nhd->htn/dot_general | solution.py:26
  66.3 1.3 %fusion.3 = f32[16,128]{1,0:T(8,128)S(1)} fusion(f32[16,128,512]{2,1,0:T(8,128)S(1)} %get-tuple-element.17, f32[16,128]{1,0:T(8,128)S(1)} %get-tuple-element.13, pred[512]{0:T(512)(128)(4,1)S(1)} %copy-done.6), kind=kLoop, calls=%fused_computation.5 | loop fusion | flops 4192256 | bytes 4211200 | tf_op jit(solution)/shard_map/reduce_sum | solution.py:33
  67.6 0.0 copy-start.2
  67.6 0.0 copy-start.5
  67.6 0.0 copy-done.4
  67.6 0.0 copy-start.1
  67.6 0.0 copy-start.3
  67.6 1.1 %fusion.16 = f32[128,16,72]{0,2,1:T(8,128)S(1)} fusion(bf16[512,16,72]{0,2,1:T(8,128)(2,1)S(1)} %bitcast.75, f32[16,128,512]{2,1,0:T(8,128)S(1)} %get-tuple-element.17, f32[16,128]{1,0:T(8,128)S(1)} %get-tuple-element.13, pred[512]{0:T(512)(128)(4,1)S(1)} %copy-done.6), kind=kOutput, calls=%fused_computation.18 | convolution fusion | flops 155189248 | bytes 5972480 | tf_op jit(solution)/shard_map/htn,nhd->thd/dot_general | solution.py:34
  68.8 0.0 copy-done.2
  68.8 0.2 fusion.24
  69.0 0.0 copy-done.5
  69.0 0.3 fusion.23
  69.3 0.0 copy-done.1
  69.4 0.5 copy-done.3
  69.9 1.3 %fusion.6 = bf16[128,1152]{1,0:T(8,128)(2,1)} fusion(bf16[128,1152]{0,1:T(8,128)(2,1)S(1)} %bitcast.76, bf16[1152,1152]{1,0:T(8,128)(2,1)S(1)} %copy-done.3, f32[1152]{0:T(1024)S(1)} %get-tuple-element.2, bf16[128,1152]{1,0:T(8,128)(2,1)S(1)} %bitcast.68), kind=kOutput, calls=%fused_computation.9 | convolution fusion | flops 340328448 | bytes 3543552 | tf_op jit(solution)/shard_map/dot_general | solution.py:93
  (6 shorter events, 0.1 us)
Async XLA Ops:
  7.2 22.0 %copy-start = (bf16[1152,1152]{1,0:T(8,128)(2,1)S(1)}, bf16[1152,1152]{1,0:T(8,128)(2,1)}, u32[]{:S(2)}) copy-start(bf16[1152,1152]{1,0:T(8,128)(2,1)} %param.8) | copy-start | bytes 7962628
  7.2 48.8 %all-gather.2.cloned.1.call-start = ((), (), s32[]{:S(2)}) async-start(), calls=%async_computation | async-start | bytes 2949120 | tf_op jit(solution)/shard_map/all_gather | solution.py:88
  56.0 8.0 %copy-start.6 = (pred[512]{0:T(512)(128)(4,1)S(1)}, pred[512]{0:T(512)(128)(4,1)}, u32[]{:S(2)}) copy-start(pred[512]{0:T(512)(128)(4,1)} %broadcast_bitcast_fusion) | copy-start | bytes 1540
  64.0 3.6 %copy-start.4 = (bf16[512,1152]{0,1:T(8,128)(2,1)S(1)}, bf16[512,1152]{0,1:T(8,128)(2,1)}, u32[]{:S(2)}) copy-start(bf16[512,1152]{0,1:T(8,128)(2,1)} %copy.29) | copy-start | bytes 3538948
  67.6 1.2 %copy-start.2 = (f32[16,128,128]{1,2,0:T(8,128)S(1)}, f32[16,128,128]{1,2,0:T(8,128)}, u32[]{:S(2)}) copy-start(f32[16,128,128]{1,2,0:T(8,128)} %get-tuple-element.15) | copy-start | bytes 3145732
  67.6 1.4 %copy-start.5 = (bf16[128,1152]{0,1:T(8,128)(2,1)S(1)}, bf16[128,1152]{0,1:T(8,128)(2,1)}, u32[]{:S(2)}) copy-start(bf16[128,1152]{0,1:T(8,128)(2,1)} %copy.22) | copy-start | bytes 884740
  67.6 1.7 %copy-start.1 = (bf16[8,16,1152]{2,1,0:T(8,128)(2,1)S(1)}, bf16[8,16,1152]{2,1,0:T(8,128)(2,1)}, u32[]{:S(2)}) copy-start(bf16[8,16,1152]{2,1,0:T(8,128)(2,1)} %param.6) | copy-start | bytes 884740
  67.6 2.2 %copy-start.3 = (bf16[1152,1152]{1,0:T(8,128)(2,1)S(1)}, bf16[1152,1152]{1,0:T(8,128)(2,1)}, u32[]{:S(2)}) copy-start(bf16[1152,1152]{1,0:T(8,128)(2,1)} %param.10) | copy-start | bytes 7962628
Sparse Core Ops, SparseCore 0:
  24.9 28.8 all-gather.1
where the time goes:
time: 78.8 us; the launch traced here: 78 us
  blocking collectives  32.4 us (41%)
  between operations  14.2 us (18%)
  local copies, waits for them, and re-layouts  13.4 us (17%)
  matrix products  11.5 us (15%)
  other arithmetic  6.48 us (8%)
    all_gather x1, blocking collectives, on_device(): groups = lax.all_gather(stale_flat[None], 'row', axis=0, tiled=True)  17.6 us
    all_gather x1, blocking collectives, on_device(): lax.all_gather(fresh_flat, 'patch', axis=0, tiled=True)  14.8 us
    unnamed x16, local copies, waits for them, and re-layouts  5.38 us
    dot_general x1, matrix products, on_device(): keyval = jnp.dot(normed, w_keyval, preferred_element_type=jnp.float32)  4.47 us
    slice x2, local copies, waits for them, and re-layouts, attend(): keys = rows[:, :width].reshape(count, HEADS, HEAD_DIM)  4.37 us
    dot_general x2, matrix products, attend(): jnp.einsum('thd,nhd->htn', queries, keys, preferred_element_type=jnp.floa...  3.66 us
    slice x2, local copies, waits for them, and re-layouts, attend(): values = rows[:, width:].reshape(count, HEADS, HEAD_DIM)  2.73 us
  transfers between devices with their start and end apart: 1, of which 0 were waited for; matrix products, arithmetic and copies ran while one was open for 21% of the time, Pallas kernels for 0%

commit v1 on v0

v1 whole, which is shorter than its diff:
```python
import functools
import math

import jax
import jax.numpy as jnp
from jax import lax
from jax.experimental import pallas as pl
from jax.experimental.pallas import tpu as pltpu
from jax.sharding import PartitionSpec as P

HEADS = 16
HEAD_DIM = 72
PAIRS = HEADS // 2
LANES = 128
WINDOW = 256
MESH = pl.DeviceIdType.MESH
F32 = jnp.float32
BF16 = jnp.bfloat16
KV_PARTS = 3
Q_PARTS = 3


def kernel(
    n_row, n_patch, grid_cols,
    tok_hbm, mod_hbm, wq_hbm, wkv_hbm, wo_hbm, stale_hbm,
    out_ref, fresh_hbm,
    tok, mod, wq, wkv, wo, kv, normed, pair_q, top, total, summed, attended,
    load_sem, kv_sem, recv_sem, first_sem, z_sem, y_sem, core_sem, fresh_sem,
):
    tokens, width = tok.shape
    block = stale_hbm.shape[0]
    n_y = n_patch // 2
    row = lax.axis_index("row")
    patch = lax.axis_index("patch")
    y_own = patch // 2
    core = patch % 2
    sibling = patch + 1 - 2 * core

    def slot(group, column):
        start = pl.multiple_of((group * n_patch + column) * block, block)
        return kv.at[pl.ds(start, block), :]

    def send(src, group, column, sem, target):
        return pltpu.make_async_remote_copy(
            src_ref=src, dst_ref=slot(group, column), send_sem=sem,
            recv_sem=recv_sem.at[group, column], device_id=target, device_id_type=MESH,
        )

    def arrived(group, column):
        pltpu.make_async_copy(
            slot(group, column), slot(group, column), recv_sem.at[group, column]
        ).wait()

    def y_column(step):
        return lax.rem(y_own + step, n_y) * 2 + core

    near = jnp.minimum(row, n_row - 1 - row)
    lower = row > n_row - 1 - row

    def order(k):
        both = k < 2 * near
        step = jnp.where(both, k // 2 + 1, k - near + 1)
        down = jnp.where(both, k % 2 == 0, lower)
        return jnp.where(down, row - step, row + step)

    loads = [
        pltpu.make_async_copy(tok_hbm, tok, load_sem.at[0]),
        pltpu.make_async_copy(mod_hbm, mod, load_sem.at[1]),
    ]
    kv_width = 2 * width // KV_PARTS
    kv_loads = [
        pltpu.make_async_copy(
            wkv_hbm.at[:, pl.ds(i * kv_width, kv_width)],
            wkv.at[:, pl.ds(i * kv_width, kv_width)],
            kv_sem.at[i],
        )
        for i in range(KV_PARTS)
    ]
    wq_load = pltpu.make_async_copy(wq_hbm, wq, load_sem.at[2])
    wo_load = pltpu.make_async_copy(wo_hbm, wo, load_sem.at[3])
    for item in loads + kv_loads + [wq_load, wo_load]:
        item.start()

    barrier = pltpu.get_barrier_semaphore()

    @pl.when(row > 0)
    def _():
        pl.semaphore_signal(barrier, inc=1, device_id={"row": row - 1}, device_id_type=MESH)

    @pl.when(row < n_row - 1)
    def _():
        pl.semaphore_signal(barrier, inc=1, device_id={"row": row + 1}, device_id_type=MESH)

    for step in range(1, n_y):
        pl.semaphore_signal(
            barrier, inc=1, device_id={"patch": y_column(step)}, device_id_type=MESH
        )
    pl.semaphore_signal(barrier, inc=1, device_id={"patch": sibling}, device_id_type=MESH)
    pl.semaphore_wait(
        barrier,
        n_y + jnp.where(row > 0, 1, 0) + jnp.where(row < n_row - 1, 1, 0),
    )

    first_down = send(stale_hbm, row, patch, first_sem.at[0], {"row": row - 1})
    first_up = send(stale_hbm, row, patch, first_sem.at[1], {"row": row + 1})

    @pl.when(row > 0)
    def _():
        first_down.start()

    @pl.when(row < n_row - 1)
    def _():
        first_up.start()

    def spread(group):
        for step in range(1, n_y):
            send(slot(group, patch), group, patch, y_sem.at[group, step],
                 {"patch": y_column(step)}).start()
        send(slot(group, patch), group, patch, core_sem.at[group, 0], {"patch": sibling}).start()

    def spread_wait(group):
        for step in range(1, n_y):
            send(slot(group, patch), group, patch, y_sem.at[group, step],
                 {"patch": y_column(step)}).wait_send()
        for step in range(n_y):
            send(slot(group, patch), group, patch, core_sem.at[group, step],
                 {"patch": sibling}).wait_send()

    def passed(k):
        group = order(k)
        target = jnp.where(group < row, row + 1, row - 1)
        copy = send(slot(group, patch), group, patch, z_sem.at[k], {"row": target})
        return group, (target >= 0) & (target < n_row), copy

    def row_event(k):
        group, inside, copy = passed(k)
        arrived(group, patch)

        @pl.when(inside)
        def _():
            copy.start()

        spread(group)

    def relay(group):
        for step in range(1, n_y):
            column = y_column(step)
            arrived(group, column)
            send(slot(group, column), group, column, core_sem.at[group, step],
                 {"patch": sibling}).start()

    def gathered(group):
        for step in range(n_y):
            arrived(group, y_column(step) + 1 - 2 * core)

    for item in loads:
        item.wait()
    values = tok[...].astype(F32)
    center = jnp.mean(values, axis=-1, keepdims=True)
    offset = values - center
    spread_sq = jnp.mean(offset * offset, axis=-1, keepdims=True)
    normal = offset * lax.rsqrt(spread_sq + 1e-06)
    normed[...] = (normal * (1.0 + mod[1:2, :]) + mod[0:1, :]).astype(BF16)

    cell = lax.broadcasted_iota(jnp.int32, (block, tokens), 0)
    token = lax.broadcasted_iota(jnp.int32, (block, tokens), 1)
    home = (token // (2 * grid_cols)) * (grid_cols // 2) + (token % grid_cols) // 2
    pool = jnp.where(home == cell, 0.25, 0.0).astype(BF16)
    pooled = jnp.dot(pool, normed[...], preferred_element_type=F32)
    coarse = pooled.astype(BF16)
    fine = (pooled - coarse.astype(F32)).astype(BF16)
    both_parts = jnp.concatenate([coarse, fine], axis=0)
    own = slot(row, patch)
    for i in range(KV_PARTS):
        kv_loads[i].wait()
        columns = pl.ds(i * kv_width, kv_width)
        product = jnp.dot(both_parts, wkv[:, columns], preferred_element_type=F32)
        own[:, columns] = (product[:block] + product[block:]).astype(BF16)
    spread(row)
    fresh_copy = pltpu.make_async_copy(own, fresh_hbm, fresh_sem)
    fresh_copy.start()

    if n_row > 1:
        row_event(0)

    wq_load.wait()
    lane = lax.broadcasted_iota(jnp.int32, (tokens, WINDOW), 1)

    def in_head(pair, which):
        begin = pair * (2 * HEAD_DIM - LANES) + which * HEAD_DIM
        return (lane >= begin) & (lane < begin + HEAD_DIM)

    query = jnp.dot(normed[...], wq[...], preferred_element_type=F32)
    for pair in range(PAIRS):
        window = query[:, pair * LANES : pair * LANES + WINDOW]
        for which in range(2):
            pair_q[pair, which * tokens : (which + 1) * tokens, :] = jnp.where(
                in_head(pair, which), window, 0.0
            ).astype(BF16)

    top[...] = jnp.full(top.shape, -1e30, F32)
    total[...] = jnp.zeros(total.shape, F32)
    summed[...] = jnp.zeros(summed.shape, F32)
    factor = math.log2(math.e) / math.sqrt(HEAD_DIM)

    def attend(start):
        rows = pl.ds(pl.multiple_of(start, LANES), LANES)
        for pair in range(PAIRS):
            keys = kv[rows, pair * LANES : pair * LANES + WINDOW]
            vals = kv[rows, width + pair * LANES : width + pair * LANES + WINDOW]
            scores = lax.dot_general(
                pair_q[pair], keys, (((1,), (1,)), ((), ())), preferred_element_type=F32
            )
            before = top[pair]
            newest = jnp.maximum(before, jnp.max(scores, axis=-1, keepdims=True))
            top[pair] = newest
            scale = jnp.exp2((before - newest) * factor)
            expo = jnp.exp2((scores - newest) * factor)
            total[pair] = total[pair] * scale + expo
            added = jnp.dot(expo.astype(BF16), vals, preferred_element_type=F32)
            summed[pair] = summed[pair] * jnp.concatenate([scale, scale], axis=1) + added

    group_rows = n_patch * block

    def step_group(q, carry):
        group = jnp.where(q == 0, row, order(jnp.maximum(q - 1, 0)))
        relay(group)

        @pl.when(q + 1 < n_row - 1)
        def _():
            row_event(q + 1)

        gathered(group)

        def step_part(u, state):
            attend(group * group_rows + u * LANES)
            return state

        return lax.fori_loop(0, group_rows // LANES, step_part, carry)

    lax.fori_loop(0, n_row, step_group, 0)

    attended[...] = jnp.zeros(attended.shape, F32)
    for pair in range(PAIRS):
        scaled = summed[pair] * (1.0 / jnp.sum(total[pair], axis=-1, keepdims=True))
        columns = slice(pair * LANES, pair * LANES + WINDOW)
        attended[:, columns] += jnp.where(
            in_head(pair, 0), scaled[:tokens], jnp.where(in_head(pair, 1), scaled[tokens:], 0.0)
        )
    wo_load.wait()
    heads = attended[...].astype(BF16)
    projected = jnp.dot(heads, wo[...], preferred_element_type=F32)
    out_ref[...] = (tok[...].astype(F32) + mod[2:3, :] * projected).astype(BF16)

    @pl.when(row > 0)
    def _():
        first_down.wait_send()

    @pl.when(row < n_row - 1)
    def _():
        first_up.wait_send()

    def finish(k, carry):
        group, inside, copy = passed(k)

        @pl.when(inside)
        def _():
            copy.wait_send()

        spread_wait(group)
        return carry

    lax.fori_loop(0, n_row - 1, finish, 0)
    spread_wait(row)
    fresh_copy.wait()


def on_device(n_row, n_patch, tokens, modulation, w_query, w_keyval, w_out, stale_kv):
    grid_rows, grid_cols, width = tokens.shape
    count = grid_rows * grid_cols
    block = count // 4
    dma = pltpu.SemaphoreType.DMA
    out, fresh = pl.pallas_call(
        functools.partial(kernel, n_row, n_patch, grid_cols),
        out_shape=(
            jax.ShapeDtypeStruct((count, width), BF16),
            jax.ShapeDtypeStruct((block, 2 * width), BF16),
        ),
        in_specs=[pl.BlockSpec(memory_space=pl.ANY)] * 6,
        out_specs=(
            pl.BlockSpec(memory_space=pltpu.VMEM),
            pl.BlockSpec(memory_space=pl.ANY),
        ),
        scratch_shapes=[
            pltpu.VMEM((count, width), BF16),
            pltpu.VMEM(modulation.shape, F32),
            pltpu.VMEM((width, width), BF16),
            pltpu.VMEM((width, 2 * width), BF16),
            pltpu.VMEM((width, width), BF16),
            pltpu.VMEM((n_row * n_patch * block, 2 * width), BF16),
            pltpu.VMEM((count, width), BF16),
            pltpu.VMEM((PAIRS, 2 * count, WINDOW), BF16),
            pltpu.VMEM((PAIRS, 2 * count, LANES), F32),
            pltpu.VMEM((PAIRS, 2 * count, LANES), F32),
            pltpu.VMEM((PAIRS, 2 * count, WINDOW), F32),
            pltpu.VMEM((count, width), F32),
            dma((4,)),
            dma((KV_PARTS,)),
            dma((n_row, n_patch)),
            dma((2,)),
            dma((n_row,)),
            dma((n_row, n_patch // 2)),
            dma((n_row, n_patch // 2)),
            dma(()),
        ],
        compiler_params=pltpu.CompilerParams(
            collective_id=0, has_side_effects=True, vmem_limit_bytes=56 * 1024 * 1024
        ),
    )(
        tokens.reshape(count, width), modulation, w_query, w_keyval, w_out,
        stale_kv.reshape(block, 2 * width),
    )
    return out.reshape(tokens.shape), fresh.reshape(stale_kv.shape)


def solution(mesh):
    tiled = P(("rep", "row"), "patch", None)
    return jax.shard_map(
        functools.partial(on_device, mesh.shape["row"], mesh.shape["patch"]),
        mesh=mesh,
        in_specs=(tiled, P(), P(), P(), P(), tiled),
        out_specs=(tiled, tiled),
        check_vma=False,
    )
```

time: 78.8 us -> 32.9 us (0.42)
  blocking collectives: 32.4 us -> 0 us
  Pallas kernels: 0 us -> 28.8 us
  between operations: 14.2 us -> 0.64 us
  matrix products: 11.5 us -> 0 us
  local copies, waits for them, and re-layouts: 13.4 us -> 3.28 us
  other arithmetic: 6.48 us -> 0 us
    all_gather x2 -> x0, blocking collectives: 32.4 us -> none  [the longest x1 17.6 us: on_device(): groups = lax.all_gather(stale_flat[None], 'row', axis=0, tiled=True)]
    pallas_call x0 -> x1, Pallas kernels: none -> 28.8 us  [on_device(): pl.pallas_call(functools.partial(kernel, n_row, n_patch, grid_cols), out_...]
    dot_general x7 -> x0, matrix products: 11.5 us -> none  [the longest x1 4.47 us: on_device(): keyval = jnp.dot(normed, w_keyval, preferred_element_type=jnp.float32)]
    slice x4 -> x0, local copies, waits for them, and re-layouts: 7.11 us -> none  [the longest x2 4.37 us: attend(): keys = rows[:, :width].reshape(count, HEADS, HEAD_DIM)]
    reduce_sum x4 -> x0, other arithmetic: 3.68 us -> none  [the longest x2 1.43 us: attend(): total = total * factor + jnp.sum(expo, axis=-1)]
    unnamed x16 -> x2, local copies, waits for them, and re-layouts: 5.38 us -> 3.28 us
    convert_element_type x3 -> x0, other arithmetic: 1.87 us -> none  [the longest x1 1.17 us: modulate(): return (normal * (1.0 + modulation[1]) + modulation[0]).astype(jnp.bfloat16)]
    slice x1 -> x0, other arithmetic: 0.88 us -> none  [on_device(): modulation[2] * projected]
  transfers between devices with their start and end apart: 1 -> 0, of which waited for: 0 -> 0; matrix products, arithmetic and copies ran while one was open for 21% -> 0% of each run, Pallas kernels for 0% -> 0%
where the time goes in v1:
time: 32.9 us; the launch traced here: 32.7 us
  Pallas kernels  28.8 us (88%)
  local copies, waits for them, and re-layouts  3.28 us (10%)
  between operations  0.64 us (2%)
    pallas_call x1, Pallas kernels, on_device(): pl.pallas_call(functools.partial(kernel, n_row, n_patch, grid_cols), out_...  28.8 us
    unnamed x2, local copies, waits for them, and re-layouts  3.28 us

profile of v1, /device:TPU:1, one launch (start us, length us, event | category | flops | bytes accessed | tf_op | source)
XLA Modules:
  0.0 32.7 jit_solution(14681240990386117734)
XLA Ops:
  0.6 28.8 %shard_map.77 = (bf16[128,1152]{1,0:T(8,128)(2,1)}, bf16[32,2304]{1,0:T(8,128)(2,1)}) custom-call(bf16[128,1152]{1,0:T(8,128)(2,1)} %bitcast.4, f32[3,1152]{1,0:T(4,128)} %mod_hbm.1, bf16[1152,1152]{1,0:T(8,128)(2,1)} %wq_hbm.1, bf16[1152,2304]{1,0:T(8,128)(2,1)} %wkv_hbm.1, bf16[1152,1152]{1,0:T(8,128)(2,1)} %wo_hbm.1, bf16[32,2304]{1,0:T(8,128)(2,1)} %bitcast.7), custom_call_target="tpu_custom_call" | custom-call | tf_op jit(solution)/shard_map/pallas_call | solution.py:283
  29.4 1.7 %copy.10 = bf16[8,16,1152]{2,1,0:T(8,128)(2,1)} copy(bf16[8,16,1152]{2,1,0:T(8,128)(2,1)} %bitcast.5) | data formatting | bytes 589824
  31.1 1.6 %copy.11 = bf16[4,8,2304]{2,1,0:T(8,128)(2,1)} copy(bf16[4,8,2304]{2,1,0:T(8,128)(2,1)} %bitcast.6) | data formatting | bytes 294912

commit v2 on v1

--- a/solution.py
+++ b/solution.py
@@ -63,6 +63,21 @@
         down = jnp.where(both, k % 2 == 0, lower)
         return jnp.where(down, row - step, row + step)
 
+    barrier = pltpu.get_barrier_semaphore()
+
+    @pl.when(row > 0)
+    def _():
+        pl.semaphore_signal(barrier, inc=1, device_id={"row": row - 1}, device_id_type=MESH)
+
+    @pl.when(row < n_row - 1)
+    def _():
+        pl.semaphore_signal(barrier, inc=1, device_id={"row": row + 1}, device_id_type=MESH)
+
+    for step in range(1, n_y):
+        pl.semaphore_signal(
+            barrier, inc=1, device_id={"patch": y_column(step)}, device_id_type=MESH
+        )
+    pl.semaphore_signal(barrier, inc=1, device_id={"patch": sibling}, device_id_type=MESH)
     loads = [
         pltpu.make_async_copy(tok_hbm, tok, load_sem.at[0]),
         pltpu.make_async_copy(mod_hbm, mod, load_sem.at[1]),
@@ -81,21 +96,6 @@
     for item in loads + kv_loads + [wq_load, wo_load]:
         item.start()
 
-    barrier = pltpu.get_barrier_semaphore()
-
-    @pl.when(row > 0)
-    def _():
-        pl.semaphore_signal(barrier, inc=1, device_id={"row": row - 1}, device_id_type=MESH)
-
-    @pl.when(row < n_row - 1)
-    def _():
-        pl.semaphore_signal(barrier, inc=1, device_id={"row": row + 1}, device_id_type=MESH)
-
-    for step in range(1, n_y):
-        pl.semaphore_signal(
-            barrier, inc=1, device_id={"patch": y_column(step)}, device_id_type=MESH
-        )
-    pl.semaphore_signal(barrier, inc=1, device_id={"patch": sibling}, device_id_type=MESH)
     pl.semaphore_wait(
         barrier,
         n_y + jnp.where(row > 0, 1, 0) + jnp.where(row < n_row - 1, 1, 0),
@@ -126,21 +126,27 @@
             send(slot(group, patch), group, patch, core_sem.at[group, step],
                  {"patch": sibling}).wait_send()
 
-    def passed(k):
-        group = order(k)
-        target = jnp.where(group < row, row + 1, row - 1)
-        copy = send(slot(group, patch), group, patch, z_sem.at[k], {"row": target})
-        return group, (target >= 0) & (target < n_row), copy
-
-    def row_event(k):
-        group, inside, copy = passed(k)
-        arrived(group, patch)
-
-        @pl.when(inside)
+    def passed(distance, sign, act):
+        group = row + sign * distance
+        target = row - sign
+
+        @pl.when((group >= 0) & (group < n_row))
         def _():
-            copy.start()
-
-        spread(group)
+            copy = send(slot(group, patch), group, patch, z_sem.at[group], {"row": target})
+            act(group, (target >= 0) & (target < n_row), copy)
+
+    def row_event(distance):
+        def act(group, inside, copy):
+            arrived(group, patch)
+
+            @pl.when(inside)
+            def _():
+                copy.start()
+
+            spread(group)
+
+        passed(distance, 1, act)
+        passed(distance, -1, act)
 
     def relay(group):
         for step in range(1, n_y):
@@ -181,7 +187,7 @@
     fresh_copy.start()
 
     if n_row > 1:
-        row_event(0)
+        row_event(1)
 
     wq_load.wait()
     lane = lax.broadcasted_iota(jnp.int32, (tokens, WINDOW), 1)
@@ -226,9 +232,9 @@
         group = jnp.where(q == 0, row, order(jnp.maximum(q - 1, 0)))
         relay(group)
 
-        @pl.when(q + 1 < n_row - 1)
+        @pl.when(q + 2 < n_row)
         def _():
-            row_event(q + 1)
+            row_event(q + 2)
 
         gathered(group)
 
@@ -260,19 +266,39 @@
     def _():
         first_up.wait_send()
 
-    def finish(k, carry):
-        group, inside, copy = passed(k)
-
-        @pl.when(inside)
-        def _():
-            copy.wait_send()
-
-        spread_wait(group)
+    def finish(distance, carry):
+        def act(group, inside, copy):
+            @pl.when(inside)
+            def _():
+                copy.wait_send()
+
+            spread_wait(group)
+
+        passed(distance, 1, act)
+        passed(distance, -1, act)
         return carry
 
-    lax.fori_loop(0, n_row - 1, finish, 0)
+    lax.fori_loop(1, n_row, finish, 0)
     spread_wait(row)
     fresh_copy.wait()
+
+
+def place(first, second, first_out, second_out, first_held, second_held, sem):
+    loads = [
+        pltpu.make_async_copy(first, first_held, sem.at[0]),
+        pltpu.make_async_copy(second, second_held, sem.at[1]),
+    ]
+    stores = [
+        pltpu.make_async_copy(first_held, first_out, sem.at[2]),
+        pltpu.make_async_copy(second_held, second_out, sem.at[3]),
+    ]
+    for item in loads:
+        item.start()
+    for load, store in zip(loads, stores):
+        load.wait()
+        store.start()
+    for item in stores:
+        item.wait()
 
 
 def on_device(n_row, n_patch, tokens, modulation, w_query, w_keyval, w_out, stale_kv):
@@ -320,6 +346,18 @@
         tokens.reshape(count, width), modulation, w_query, w_keyval, w_out,
         stale_kv.reshape(block, 2 * width),
     )
+    hbm = pl.BlockSpec(memory_space=pl.ANY)
+    out, fresh = pl.pallas_call(
+        place,
+        out_shape=(
+            jax.ShapeDtypeStruct(out.shape, BF16),
+            jax.ShapeDtypeStruct(fresh.shape, BF16),
+        ),
+        in_specs=[hbm, hbm],
+        out_specs=(hbm, hbm),
+        scratch_shapes=[pltpu.VMEM(out.shape, BF16), pltpu.VMEM(fresh.shape, BF16), dma((4,))],
+        compiler_params=pltpu.CompilerParams(vmem_limit_bytes=56 * 1024 * 1024),
+    )(out, fresh)
     return out.reshape(tokens.shape), fresh.reshape(stale_kv.shape)
 
 

time: 32.9 us -> 28.9 us (0.88)
  local copies, waits for them, and re-layouts: 3.28 us -> 0 us
  Pallas kernels: 28.8 us -> 28.1 us
    unnamed x2 -> x0, local copies, waits for them, and re-layouts: 3.28 us -> none
    pallas_call x1, Pallas kernels: 28.8 us -> 26.4 us  [on_device(): pl.pallas_call(functools.partial(kernel, n_row, n_patch, grid_cols), out_...]
    pallas_call x0 -> x1, Pallas kernels: none -> 1.75 us  [on_device(): pl.pallas_call(place, out_shape=(jax.ShapeDtypeStruct(out.shape, BF16), j...]
where the time goes in v2:
time: 28.9 us; the launch traced here: 28.8 us
  Pallas kernels  28.1 us (97%)
  between operations  0.64 us (2%)
    pallas_call x1, Pallas kernels, on_device(): pl.pallas_call(functools.partial(kernel, n_row, n_patch, grid_cols), out_...  26.4 us
    pallas_call x1, Pallas kernels, on_device(): pl.pallas_call(place, out_shape=(jax.ShapeDtypeStruct(out.shape, BF16), j...  1.75 us

profile of v2, /device:TPU:1, one launch (start us, length us, event | category | flops | bytes accessed | tf_op | source)
XLA Modules:
  0.0 28.8 jit_solution(1811164475935226327)
XLA Ops:
  0.6 26.4 %shard_map.77 = (bf16[128,1152]{1,0:T(8,128)(2,1)}, bf16[32,2304]{1,0:T(8,128)(2,1)}) custom-call(bf16[128,1152]{1,0:T(8,128)(2,1)} %bitcast.4, f32[3,1152]{1,0:T(4,128)} %mod_hbm.1, bf16[1152,1152]{1,0:T(8,128)(2,1)} %wq_hbm.1, bf16[1152,2304]{1,0:T(8,128)(2,1)} %wkv_hbm.1, bf16[1152,1152]{1,0:T(8,128)(2,1)} %wo_hbm.1, bf16[32,2304]{1,0:T(8,128)(2,1)} %bitcast.5), custom_call_target="tpu_custom_call" | custom-call | tf_op jit(solution)/shard_map/pallas_call | solution.py:309
  27.0 1.8 %shard_map.78 = (bf16[128,1152]{1,0:T(8,128)(2,1)}, bf16[32,2304]{1,0:T(8,128)(2,1)}) custom-call(bf16[128,1152]{1,0:T(8,128)(2,1)} %get-tuple-element.6.first, bf16[32,2304]{1,0:T(8,128)(2,1)} %get-tuple-element.7.second), custom_call_target="tpu_custom_call" | custom-call | tf_op jit(solution)/shard_map/pallas_call | solution.py:350

commit v3 on v2

--- a/solution.py
+++ b/solution.py
@@ -17,7 +17,6 @@
 F32 = jnp.float32
 BF16 = jnp.bfloat16
 KV_PARTS = 3
-Q_PARTS = 3
 
 
 def kernel(
@@ -25,7 +24,7 @@
     tok_hbm, mod_hbm, wq_hbm, wkv_hbm, wo_hbm, stale_hbm,
     out_ref, fresh_hbm,
     tok, mod, wq, wkv, wo, kv, normed, pair_q, top, total, summed, attended,
-    load_sem, kv_sem, recv_sem, first_sem, z_sem, y_sem, core_sem, fresh_sem,
+    cross, load_sem, kv_sem, recv_sem, key_sem, cross_recv, cross_send, pass_sem, first_sem, z_sem, y_sem, core_sem, fresh_sem,
 ):
     tokens, width = tok.shape
     block = stale_hbm.shape[0]
@@ -50,6 +49,41 @@
         pltpu.make_async_copy(
             slot(group, column), slot(group, column), recv_sem.at[group, column]
         ).wait()
+
+    def half(ref, which):
+        return ref.at[:, pl.ds(which * width, width)]
+
+    def cross_send_copy(step):
+        return pltpu.make_async_remote_copy(
+            src_ref=half(stale_hbm, 0), dst_ref=cross.at[y_own], send_sem=cross_send.at[step],
+            recv_sem=cross_recv.at[y_own], device_id={"patch": y_column(step)},
+            device_id_type=MESH,
+        )
+
+    def cross_pass(step, target, which):
+        column = y_column(step)
+        return pltpu.make_async_remote_copy(
+            src_ref=cross.at[column // 2], dst_ref=half(slot(row, column), 0),
+            send_sem=pass_sem.at[which, step], recv_sem=key_sem.at[row, column],
+            device_id={"row": target}, device_id_type=MESH,
+        )
+
+    def cross_event(act):
+        for step in range(1, n_y):
+            @pl.when(row > 0)
+            def _(step=step):
+                act(cross_pass(step, row - 1, 0))
+
+            @pl.when(row < n_row - 1)
+            def _(step=step):
+                act(cross_pass(step, row + 1, 1))
+
+    def cross_arrived():
+        for step in range(1, n_y):
+            source = y_column(step) // 2
+            pltpu.make_async_copy(
+                cross.at[source], cross.at[source], cross_recv.at[source]
+            ).wait()
 
     def y_column(step):
         return lax.rem(y_own + step, n_y) * 2 + core
@@ -93,7 +127,7 @@
     ]
     wq_load = pltpu.make_async_copy(wq_hbm, wq, load_sem.at[2])
     wo_load = pltpu.make_async_copy(wo_hbm, wo, load_sem.at[3])
-    for item in loads + kv_loads + [wq_load, wo_load]:
+    for item in loads:
         item.start()
 
     pl.semaphore_wait(
@@ -101,27 +135,46 @@
         n_y + jnp.where(row > 0, 1, 0) + jnp.where(row < n_row - 1, 1, 0),
     )
 
-    first_down = send(stale_hbm, row, patch, first_sem.at[0], {"row": row - 1})
-    first_up = send(stale_hbm, row, patch, first_sem.at[1], {"row": row + 1})
-
-    @pl.when(row > 0)
-    def _():
-        first_down.start()
-
-    @pl.when(row < n_row - 1)
-    def _():
-        first_up.start()
-
-    def spread(group):
+    def z_copy(src, group, which, sem, target):
+        return pltpu.make_async_remote_copy(
+            src_ref=half(src, which), dst_ref=half(slot(group, patch), which), send_sem=sem,
+            recv_sem=(key_sem, recv_sem)[which].at[group, patch], device_id={"row": target},
+            device_id_type=MESH,
+        )
+
+    def first_event(act):
+        for which in range(2):
+            @pl.when(row > 0)
+            def _(which=which):
+                act(z_copy(stale_hbm, row, which, first_sem.at[0, which], row - 1))
+
+            @pl.when(row < n_row - 1)
+            def _(which=which):
+                act(z_copy(stale_hbm, row, which, first_sem.at[1, which], row + 1))
+
+    first_event(lambda copy: copy.start())
+
+    for step in range(1, n_y):
+        cross_send_copy(step).start()
+
+    def y_send(group, step, adjacent):
+        part = slot(group, patch)
+        if adjacent:
+            part = half(part, 1)
+        return pltpu.make_async_remote_copy(
+            src_ref=part, dst_ref=part, send_sem=y_sem.at[group, step],
+            recv_sem=recv_sem.at[group, patch], device_id={"patch": y_column(step)},
+            device_id_type=MESH,
+        )
+
+    def spread(group, adjacent=False):
         for step in range(1, n_y):
-            send(slot(group, patch), group, patch, y_sem.at[group, step],
-                 {"patch": y_column(step)}).start()
+            y_send(group, step, adjacent).start()
         send(slot(group, patch), group, patch, core_sem.at[group, 0], {"patch": sibling}).start()
 
-    def spread_wait(group):
+    def spread_wait(group, adjacent=False):
         for step in range(1, n_y):
-            send(slot(group, patch), group, patch, y_sem.at[group, step],
-                 {"patch": y_column(step)}).wait_send()
+            y_send(group, step, adjacent).wait_send()
         for step in range(n_y):
             send(slot(group, patch), group, patch, core_sem.at[group, step],
                  {"patch": sibling}).wait_send()
@@ -132,18 +185,24 @@
 
         @pl.when((group >= 0) & (group < n_row))
         def _():
-            copy = send(slot(group, patch), group, patch, z_sem.at[group], {"row": target})
-            act(group, (target >= 0) & (target < n_row), copy)
-
-    def row_event(distance):
-        def act(group, inside, copy):
-            arrived(group, patch)
-
-            @pl.when(inside)
-            def _():
-                copy.start()
-
-            spread(group)
+            act(group, (target >= 0) & (target < n_row), [
+                z_copy(slot(group, patch), group, which, z_sem.at[group, which], target)
+                for which in range(2)
+            ])
+
+    def row_event(distance, adjacent=False):
+        def act(group, inside, copies):
+            for which in range(2):
+                part = half(slot(group, patch), which)
+                pltpu.make_async_copy(
+                    part, part, (key_sem, recv_sem)[which].at[group, patch]
+                ).wait()
+
+                @pl.when(inside)
+                def _(which=which):
+                    copies[which].start()
+
+            spread(group, adjacent)
 
         passed(distance, 1, act)
         passed(distance, -1, act)
@@ -151,13 +210,28 @@
     def relay(group):
         for step in range(1, n_y):
             column = y_column(step)
-            arrived(group, column)
+            adjacent = (group == row - 1) | (group == row + 1)
+
+            @pl.when(adjacent)
+            def _(column=column):
+                part = half(slot(group, column), 1)
+                pltpu.make_async_copy(part, part, recv_sem.at[group, column]).wait()
+                part = half(slot(group, column), 0)
+                pltpu.make_async_copy(part, part, key_sem.at[group, column]).wait()
+
+            @pl.when(jnp.logical_not(adjacent))
+            def _(column=column):
+                arrived(group, column)
+
             send(slot(group, column), group, column, core_sem.at[group, step],
                  {"patch": sibling}).start()
 
     def gathered(group):
         for step in range(n_y):
             arrived(group, y_column(step) + 1 - 2 * core)
+
+    for item in kv_loads + [wq_load, wo_load]:
+        item.start()
 
     for item in loads:
         item.wait()
@@ -178,6 +252,9 @@
     both_parts = jnp.concatenate([coarse, fine], axis=0)
     own = slot(row, patch)
     for i in range(KV_PARTS):
+        if i == 2:
+            cross_arrived()
+            cross_event(lambda copy: copy.start())
         kv_loads[i].wait()
         columns = pl.ds(i * kv_width, kv_width)
         product = jnp.dot(both_parts, wkv[:, columns], preferred_element_type=F32)
@@ -187,7 +264,7 @@
     fresh_copy.start()
 
     if n_row > 1:
-        row_event(1)
+        row_event(1, True)
 
     wq_load.wait()
     lane = lax.broadcasted_iota(jnp.int32, (tokens, WINDOW), 1)
@@ -230,11 +307,17 @@
 
     def step_group(q, carry):
         group = jnp.where(q == 0, row, order(jnp.maximum(q - 1, 0)))
-        relay(group)
+        @pl.when(q > 0)
+        def _():
+            relay(group)
 
         @pl.when(q + 2 < n_row)
         def _():
             row_event(q + 2)
+
+        @pl.when(q == 0)
+        def _():
+            relay(group)
 
         gathered(group)
 
@@ -258,27 +341,27 @@
     projected = jnp.dot(heads, wo[...], preferred_element_type=F32)
     out_ref[...] = (tok[...].astype(F32) + mod[2:3, :] * projected).astype(BF16)
 
-    @pl.when(row > 0)
-    def _():
-        first_down.wait_send()
-
-    @pl.when(row < n_row - 1)
-    def _():
-        first_up.wait_send()
-
-    def finish(distance, carry):
-        def act(group, inside, copy):
+    first_event(lambda copy: copy.wait_send())
+
+    def finish(distance, carry, adjacent=False):
+        def act(group, inside, copies):
             @pl.when(inside)
             def _():
-                copy.wait_send()
-
-            spread_wait(group)
+                for copy in copies:
+                    copy.wait_send()
+
+            spread_wait(group, adjacent)
 
         passed(distance, 1, act)
         passed(distance, -1, act)
         return carry
 
-    lax.fori_loop(1, n_row, finish, 0)
+    if n_row > 1:
+        finish(1, 0, True)
+    lax.fori_loop(2, n_row, finish, 0)
+    for step in range(1, n_y):
+        cross_send_copy(step).wait_send()
+    cross_event(lambda copy: copy.wait_send())
     spread_wait(row)
     fresh_copy.wait()
 
@@ -330,11 +413,16 @@
             pltpu.VMEM((PAIRS, 2 * count, LANES), F32),
             pltpu.VMEM((PAIRS, 2 * count, WINDOW), F32),
             pltpu.VMEM((count, width), F32),
+            pltpu.VMEM((n_patch // 2, block, width), BF16),
             dma((4,)),
             dma((KV_PARTS,)),
             dma((n_row, n_patch)),
-            dma((2,)),
-            dma((n_row,)),
+            dma((n_row, n_patch)),
+            dma((n_patch // 2,)),
+            dma((n_patch // 2,)),
+            dma((2, n_patch // 2)),
+            dma((2, 2)),
+            dma((n_row, 2)),
             dma((n_row, n_patch // 2)),
             dma((n_row, n_patch // 2)),
             dma(()),

time: 28.9 us -> 28.7 us (level)
  no operation moved by 1% of the time
where the time goes in v3:
time: 28.7 us; the launch traced here: 28.6 us
  Pallas kernels  28 us (98%)
  between operations  0.64 us (2%)
    pallas_call x1, Pallas kernels, on_device(): pl.pallas_call(functools.partial(kernel, n_row, n_patch, grid_cols), out_...  26.2 us
    pallas_call x1, Pallas kernels, on_device(): pl.pallas_call(place, out_shape=(jax.ShapeDtypeStruct(out.shape, BF16), j...  1.75 us

profile of v3, /device:TPU:1, one launch (start us, length us, event | category | flops | bytes accessed | tf_op | source)
XLA Modules:
  0.0 28.6 jit_solution(10301530807378932009)
XLA Ops:
  0.6 26.2 %shard_map.77 = (bf16[128,1152]{1,0:T(8,128)(2,1)}, bf16[32,2304]{1,0:T(8,128)(2,1)}) custom-call(bf16[128,1152]{1,0:T(8,128)(2,1)} %bitcast.4, f32[3,1152]{1,0:T(4,128)} %mod_hbm.1, bf16[1152,1152]{1,0:T(8,128)(2,1)} %wq_hbm.1, bf16[1152,2304]{1,0:T(8,128)(2,1)} %wkv_hbm.1, bf16[1152,1152]{1,0:T(8,128)(2,1)} %wo_hbm.1, bf16[32,2304]{1,0:T(8,128)(2,1)} %bitcast.5), custom_call_target="tpu_custom_call" | custom-call | tf_op jit(solution)/shard_map/pallas_call | solution.py:392
  26.8 1.8 %shard_map.78 = (bf16[128,1152]{1,0:T(8,128)(2,1)}, bf16[32,2304]{1,0:T(8,128)(2,1)}) custom-call(bf16[128,1152]{1,0:T(8,128)(2,1)} %get-tuple-element.6.first, bf16[32,2304]{1,0:T(8,128)(2,1)} %get-tuple-element.7.second), custom_call_target="tpu_custom_call" | custom-call | tf_op jit(solution)/shard_map/pallas_call | solution.py:438
